TPU v7x, 32 devices: a whole 2x2x4 slice. The times are simulated.
32 devices in a mesh: req: 8 (over z, x), tp: 4 (over y, core).
Axes of the slice: x: 2, y: 2, z: 4, core: 2. Of those that a mesh axis runs over, the one named last changes fastest.
Arguments:
- layer_in: bfloat16 [4, 64, 2880], P(None, 'req'), may hold values from -3 to 3
- query_in: bfloat16 [4, 64, 2048], P(None, 'req', 'tp'), may hold values from -6 to 6
- unrotated_key: bfloat16 [4, 64, 512], P(None, 'req', 'tp'), may hold values from -6 to 6
- incoming_value: bfloat16 [4, 64, 512], P(None, 'req', 'tp'), may hold values from -12 to 12
- rotated_prompt_keys: bfloat16 [64, 256, 512], P('req', None, 'tp'), may hold values from -270 to 270
- prompt_value_rows: bfloat16 [64, 256, 512], P('req', None, 'tp'), may hold values from -6 to 6
- generated_key_rows: bfloat16 [64, 64, 512], P('req', None, 'tp'), may hold values from -9 to 9
- generated_value_rows: bfloat16 [64, 64, 512], P('req', None, 'tp'), may hold values from -12 to 12
- lengths: int32 [8], replicated, may hold values from 128 to 2048, as said below
- parents: int32 [4, 8, 8], replicated, may hold values from 0 to 7
- routes: int32 [4, 64, 4], P(None, 'req'), may hold values from 0 to 15, all different within a row; in each aligned block of 8 rows (0 to 7, 8 to 15, ..., all dimensions but the last counted through in order) at most 4 rows name the same one
- head_sink_logits: float32 [32], P('tp'), may hold values from 1 to 6
- out_weight: bfloat16 [2048, 2880], P('tp'), may hold values from -0.5 to 0.5
- mlp_gain: float32 [2880], replicated, may hold values from 0.5 to 1.5
- router_weight: bfloat16 [2880, 16], replicated, may hold values from -0.21875 to 0.21875
- expert_gate: bfloat16 [16, 2880, 2880], P('req', None, 'tp'), may hold values from -0.4375 to 0.4375
- expert_up: bfloat16 [16, 2880, 2880], P('req', None, 'tp'), may hold values from -0.4375 to 0.4375
- expert_down: bfloat16 [16, 2880, 2880], P('req', 'tp'), may hold values from -0.109375 to 0.109375
- next_gain: float32 [2880], replicated, may hold values from 0.5 to 1.5
- next_q_weight: bfloat16 [2880, 2048], P(None, 'tp'), may hold values from -0.109375 to 0.109375
- following_key_value_weight: bfloat16 [2880, 2, 512], P(None, None, 'tp'), may hold values from -0.109375 to 0.109375
Outputs:
- layer_out: bfloat16 [4, 64, 2880], P(None, 'req')
- next_query: bfloat16 [4, 64, 2048], P(None, 'req', 'tp')
- next_keyval: bfloat16 [4, 64, 2, 512], P(None, 'req', None, 'tp')
Inputs may be any that keep to these rules, and one draw needn't show every extreme that they name: `lengths`: some group's prompt holds exactly 2048 positions. `routes`: a row names 4 different experts; in the rows of one device at one step no expert is named more than 4 times, a bound that some block reaches.
All inputs are finite; a program needn't handle non-finite values.
Results may differ from a plain program's by a relative error of at most 0.029.
Values may be sent and summed in bfloat16 or wider, within the bound.
A program may use at most 128 MiB of HBM per device.

v0:
```python
import jax
import jax.numpy as jnp
from jax import lax
from jax.sharding import PartitionSpec as P

HEAD = 64
EXPERTS = 16
THETA = 150000.0
EPS = 1e-05
NEG = -1e30
BF = jnp.bfloat16
F32 = jnp.float32


def rope(vectors, positions):
    half = HEAD // 2
    powers = jnp.arange(half, dtype=F32) * (2.0 / HEAD)
    angles = positions.astype(F32)[..., None, None] * jnp.power(THETA, -powers)
    cos, sin = (jnp.cos(angles), jnp.sin(angles))
    lower, upper = (vectors[..., :half], vectors[..., half:])
    return jnp.concatenate([lower * cos - upper * sin, lower * sin + upper * cos], axis=-1)


def rms(rows, gain):
    return rows * lax.rsqrt(jnp.mean(rows * rows, axis=-1, keepdims=True) + EPS) * gain


def lineage_tables(parents):
    steps, groups, beams = parents.shape
    ident = jnp.broadcast_to(jnp.arange(beams, dtype=jnp.int32), (groups, beams))
    first = []
    tokens = [[None] * steps for _ in range(steps)]
    for t in range(steps):
        walker = ident
        for s in range(t, -1, -1):
            tokens[s][t] = walker
            hot = walker[..., None] == jnp.arange(beams, dtype=jnp.int32)
            walker = jnp.sum(jnp.where(hot, parents[s][:, None, :], 0), axis=-1)
        first.append(walker)
        for s in range(t + 1, steps):
            tokens[s][t] = jnp.full_like(ident, -1)
    return (jnp.stack(first), jnp.stack([jnp.stack(row) for row in tokens]))


def local(
    layer_in,
    query_in,
    key_in,
    value_in,
    prompt_keys,
    prompt_values,
    gen_keys,
    gen_values,
    lengths,
    parents,
    routes,
    sinks,
    out_weight,
    mlp_gain,
    router_weight,
    expert_gate,
    expert_up,
    expert_down,
    next_gain,
    next_q_weight,
    next_kv_weight,
):
    req_count = lax.axis_size("req")
    me = lax.axis_index("req")
    T, B, q_width = query_in.shape
    kv_width = key_in.shape[2]
    K = kv_width // HEAD
    R = q_width // kv_width
    J = parents.shape[2]
    span = req_count // J
    beam = me // span
    start = me % span * B
    groups = [[c + span * j for j in range(J)] for c in range(span)]
    if span == 1:
        groups = None
    lens = lax.dynamic_slice_in_dim(lengths, start, B)
    pars = lax.dynamic_slice_in_dim(parents, start, B, axis=1)
    S = prompt_keys.shape[1]
    G = gen_keys.shape[1]
    pos = lens[None, :] + G + jnp.arange(T, dtype=jnp.int32)[:, None]
    q = rope(query_in.astype(F32).reshape(T, B, K * R, HEAD), pos).astype(BF).reshape(T, B, q_width)
    k = rope(key_in.astype(F32).reshape(T, B, K, HEAD), pos).astype(BF).reshape(T, B, kv_width)
    q_all = lax.all_gather(q, "req", axis_index_groups=groups)
    first, tokens = lineage_tables(pars)
    prompt_ok = (beam * S + jnp.arange(S, dtype=jnp.int32))[None, :] < lens[:, None]
    mask = jnp.concatenate(
        [
            jnp.broadcast_to(prompt_ok[:, None, None, :], (B, J, T, S)),
            jnp.broadcast_to((first == beam).transpose(1, 2, 0)[..., None], (B, J, T, G)),
            (tokens == beam).transpose(2, 3, 1, 0),
        ],
        axis=-1,
    )
    keys = jnp.concatenate([prompt_keys, gen_keys, k.transpose(1, 0, 2)], axis=1)
    values = jnp.concatenate([prompt_values, gen_values, value_in.transpose(1, 0, 2)], axis=1)
    keys = keys.reshape(B, S + G + T, K, HEAD)
    values = values.reshape(B, S + G + T, K, HEAD)
    qs = q_all.reshape(J, T, B, K, R, HEAD)
    scores = jnp.einsum("jtbkrd,bskd->bkjtrs", qs, keys, preferred_element_type=F32) * 0.125
    usable = mask[:, None, :, :, None, :]
    scores = jnp.where(usable, scores, NEG)
    high = jnp.max(scores, axis=-1)
    weights = jnp.where(usable, jnp.exp(scores - high[..., None]), 0.0)
    total = jnp.sum(weights, axis=-1)
    part = jnp.einsum("bkjtrs,bskd->jtbkrd", weights.astype(BF), values, preferred_element_type=F32)
    high = high.transpose(2, 3, 0, 1, 4)
    total = total.transpose(2, 3, 0, 1, 4)
    part = (part / jnp.maximum(total, 1e-30)[..., None]).astype(BF)
    stats = jnp.stack([high, total], axis=1)
    part = lax.all_to_all(part, "req", 0, 0, axis_index_groups=groups)
    stats = lax.all_to_all(stats, "req", 0, 0, axis_index_groups=groups)
    high, total = (stats[:, 0], stats[:, 1])
    sink = sinks.reshape(K, R)
    peak = jnp.maximum(jnp.max(high, axis=0), sink)
    share = total * jnp.exp(high - peak)
    bottom = jnp.sum(share, axis=0) + jnp.exp(sink - peak)
    attended = jnp.sum(part.astype(F32) * (share / bottom)[..., None], axis=0)
    attended = attended.astype(BF).reshape(T * B, q_width)
    projected = jnp.dot(attended, out_weight, preferred_element_type=F32)
    x1 = layer_in.reshape(T * B, -1).astype(F32) + lax.psum(projected.astype(BF), "tp").astype(F32)
    h2 = rms(x1, mlp_gain).astype(BF)
    logits = jnp.dot(h2, router_weight, preferred_element_type=F32)
    hot = jnp.sum(
        (routes.reshape(T * B, -1, 1) == jnp.arange(EXPERTS, dtype=jnp.int32)).astype(F32), axis=1
    )
    masked = jnp.where(hot > 0, logits, NEG)
    raw = jnp.where(hot > 0, jnp.exp(masked - jnp.max(masked, axis=-1, keepdims=True)), 0.0)
    gates = raw / jnp.sum(raw, axis=-1, keepdims=True)
    h2_all = lax.all_gather(h2, "req", tiled=True)
    gates_all = lax.all_gather(gates, "req", tiled=True)
    slabs = expert_gate.shape[0]
    split = slabs * req_count // EXPERTS
    moe = 0.0
    for s in range(slabs):
        expert = (me * slabs + s) // split
        weight = lax.dynamic_slice_in_dim(gates_all, expert, 1, axis=1)
        gate = jnp.minimum(jnp.dot(h2_all, expert_gate[s], preferred_element_type=F32), 7.0)
        up = jnp.clip(jnp.dot(h2_all, expert_up[s], preferred_element_type=F32), -7.0, 7.0)
        hidden = ((up + 1.0) * gate * jax.nn.sigmoid(1.702 * gate) * weight).astype(BF)
        moe = moe + jnp.dot(hidden, expert_down[s], preferred_element_type=F32)
    moe = lax.psum_scatter(moe.astype(BF), "req", scatter_dimension=0, tiled=True)
    moe = lax.psum(moe, "tp").astype(F32)
    x2 = x1 + moe
    h3 = rms(x2, next_gain).astype(BF)
    next_query = jnp.dot(h3, next_q_weight, preferred_element_type=F32).astype(BF)
    next_kv = jnp.einsum("nd,dcf->ncf", h3, next_kv_weight, preferred_element_type=F32).astype(BF)
    return (
        x2.astype(BF).reshape(T, B, -1),
        next_query.reshape(T, B, q_width),
        next_kv.reshape(T, B, 2, kv_width),
    )


def solution(mesh):
    placed = (
        P(None, "req", None),
        P(None, "req", "tp"),
        P(None, "req", "tp"),
        P(None, "req", "tp"),
        P("req", None, "tp"),
        P("req", None, "tp"),
        P("req", None, "tp"),
        P("req", None, "tp"),
        P(),
        P(),
        P(None, "req", None),
        P("tp"),
        P("tp", None),
        P(),
        P(),
        P("req", None, "tp"),
        P("req", None, "tp"),
        P("req", "tp", None),
        P(),
        P(None, "tp"),
        P(None, None, "tp"),
    )
    return jax.shard_map(
        local,
        mesh=mesh,
        in_specs=placed,
        out_specs=(P(None, "req", None), P(None, "req", "tp"), P(None, "req", None, "tp")),
        check_vma=False,
    )
```

profile of v0, /device:TPU:0, one launch (start us, length us, event | category | flops | bytes accessed | tf_op | source)
XLA Modules:
  0.0 316.0 jit_solution(11140793845565401066)
XLA Ops:
  7.2 0.8 broadcast_add_fusion
  8.0 0.8 broadcast_compare_fusion.1
  8.8 0.7 slice_bitcast_fusion.4
  10.1 0.5 select_reduce_fusion.8
  10.7 0.7 select_reduce_fusion.9
  12.0 0.8 reshape.192
  13.1 0.9 reshape.190
  14.3 34.5 %all_gather.9 = bf16[8,4,8,512]{3,2,1,0:T(8,128)(2,1)} all-gather(bf16[1,4,8,512]{3,2,1,0:T(8,128)(2,1)S(1)} %convert_element_type.87), channel_id=1, replica_groups=mesh['req'=8,'tp'=4] {'req'}, dimensions={0}, use_global_device_ids=true | all-gather | bytes 294912 | tf_op jit(solution)/shard_map/all_gather | solution.py:88
  48.8 1.3 reshape.181
  50.1 2.0 pad_maximum_fusion.1
  52.1 2.2 copy.122
  54.6 2.0 fusion.24
  56.7 1.6 copy-done.1
  58.3 1.3 fusion.25
  59.6 0.8 pad_maximum_fusion.2
  60.4 1.3 copy.125
  61.7 0.9 reshape.201
  62.6 5.5 %all-to-all-start.1 = ((f32[8,1,512]{2,1,0:T(1,128)}), f32[8,1,512]{2,1,0:T(1,128)S(1)}, u32[]{:S(2)}, u32[]{:S(2)}) async-start(f32[8,1,512]{2,1,0:T(1,128)} %reshape.201), calls=%async_computation.1 | async-start | bytes 32768 | tf_op jit(solution)/shard_map/all_to_all | solution.py:116
  68.1 2.0 pad_maximum_fusion
  70.1 2.2 copy.115
  72.4 3.9 %divide_convert_fusion = bf16[8,4,8,2,4,64]{5,0,4,1,3,2:T(8,128)(2,1)} fusion(bf16[8,324,2,64,1,1]{1,3,5,4,2,0:T(8,128)(2,1)} %bitcast.191, f32[8,2,8,4,4,324]{5,2,4,3,1,0:T(8,128)} %copy-done.1, f32[8,2,8,4,4]{2,4,3,1,0:T(4,128)S(1)} %copy-done.6, pred[8,8,4,324]{3,1,2,0:T(8,128)(4,1)} %copy-done.7, f32[8,4,8,2,4]{0,4,1,3,2:T(4,128)S(1)} %bitcast_maximum_fusion), kind=kOutput, calls=%fused_computation.55 | convolution fusion | flops 88514560 | bytes 3679232 | tf_op jit(solution)/shard_map/bkjtrs,bskd->jtbkrd/dot_general | solution.py:110
  76.3 1.2 copy.157
  77.6 1.1 reshape.199
  78.7 6.0 %all-to-all-start = ((bf16[8,2,8192]{2,1,0:T(2,128)(2,1)}), bf16[8,2,8192]{2,1,0:T(2,128)(2,1)}, u32[]{:S(2)}, u32[]{:S(2)}) async-start(bf16[8,2,8192]{2,1,0:T(2,128)(2,1)} %reshape.199), calls=%async_computation | async-start | bytes 524288 | tf_op jit(solution)/shard_map/all_to_all | solution.py:115
  84.7 0.5 broadcast.189
  85.2 0.7 reduce.1
  86.6 0.5 copy.127
  87.1 5.9 %all-to-all-done = bf16[8,2,8192]{2,1,0:T(2,128)(2,1)} async-done(((bf16[8,2,8192]{2,1,0:T(2,128)(2,1)}), bf16[8,2,8192]{2,1,0:T(2,128)(2,1)}, u32[]{:S(2)}, u32[]{:S(2)}) %all-to-all-start) | async-done | bytes 262176 | tf_op jit(solution)/shard_map/all_to_all | solution.py:115
  93.0 2.1 reshape.200
  95.1 1.7 multiply_reduce_fusion
  97.0 1.6 convolution_convert_fusion
  98.7 29.9 %all-reduce.3.cloned.1.call-done = bf16[32,2880]{1,0:T(8,128)(2,1)} async-done(((bf16[32,2880]{1,0:T(8,128)(2,1)}), bf16[32,2880]{1,0:T(8,128)(2,1)}) %all-reduce.3.cloned.1.call-update) | async-done | bytes 184336 | tf_op jit(solution)/shard_map/psum | solution.py:125
  128.6 1.1 multiply_reduce_fusion.2
  129.8 1.7 multiply_convert_fusion.1
  131.7 1.1 fusion.121
  132.8 30.8 %all-gather = f32[8,32,16]{1,2,0:T(8,128)S(1)} all-gather(f32[1,32,16]{1,2,0:T(8,128)S(1)} %divide_bitcast_fusion), channel_id=1, replica_groups=mesh['req'=8,'tp'=4] {'req'}, dimensions={0}, use_global_device_ids=true | all-gather | bytes 18432 | tf_op jit(solution)/shard_map/all_gather | solution.py:135
  163.8 11.5 %all-gather.3.cloned.1.call-done = bf16[256,2880]{1,0:T(8,128)(2,1)} async-done(((bf16[32,2880]{1,0:T(8,128)(2,1)}), bf16[256,2880]{1,0:T(8,128)(2,1)}) %all-gather.3.cloned.1.call-update) | async-done | bytes 1474576 | tf_op jit(solution)/shard_map/all_gather | solution.py:134
  175.3 5.0 %fusion.48 = f32[256,720]{0,1:T(8,128)} fusion(bf16[256,2880]{1,0:T(8,128)(2,1)} %all-gather.3.cloned.1.call-done, bf16[2,2880,720]{1,2,0:T(8,128)(2,1)} %param.36), kind=kOutput, calls=%fused_computation.38 | convolution fusion | flops 1061867520 | bytes 6483968 | tf_op jit(solution)/shard_map/dot_general | solution.py:142
  180.3 4.4 %fusion.42 = f32[256,720]{0,1:T(8,128)} fusion(bf16[256,2880]{1,0:T(8,128)(2,1)S(1)} %copy-done.13, bf16[2,2880,720]{1,2,0:T(8,128)(2,1)} %param.36), kind=kOutput, calls=%fused_computation.36 | convolution fusion | flops 1061867520 | bytes 6451200 | tf_op jit(solution)/shard_map/dot_general | solution.py:142
  184.7 10.7 %fusion = f32[256,2880]{1,0:T(8,128)} fusion(bf16[2,720,2880]{2,1,0:T(8,128)(2,1)} %param.38, f32[256,720]{0,1:T(8,128)} %fusion.48, bf16[256,2880]{1,0:T(8,128)(2,1)} %all-gather.3.cloned.1.call-done, bf16[2,2880,720]{1,2,0:T(8,128)(2,1)} %param.37, f32[256]{0:T(256)S(1)} %bitcast.205), kind=kOutput, calls=%fused_computation | convolution fusion | flops 2125209600 | bytes 13673472 | tf_op jit(solution)/shard_map/dot_general | solution.py:145
  195.3 11.1 %fusion.21 = bf16[256,2880]{1,0:T(8,128)(2,1)} fusion(f32[256,2880]{1,0:T(8,128)} %fusion, bf16[2,720,2880]{2,1,0:T(8,128)(2,1)} %param.38, f32[256,720]{0,1:T(8,128)} %fusion.42, bf16[256,2880]{1,0:T(8,128)(2,1)} %all-gather.3.cloned.1.call-done, bf16[2,2880,720]{1,2,0:T(8,128)(2,1)} %param.37, f32[256]{0:T(256)S(1)} %bitcast.204), kind=kOutput, calls=%fused_computation.19 | convolution fusion | flops 2126684160 | bytes 15213568 | tf_op jit(solution)/shard_map/dot_general | solution.py:145
  206.5 63.7 %reduce-scatter.2.cloned.1.call-done = bf16[32,2880]{1,0:T(8,128)(2,1)} async-done(((bf16[256,2880]{1,0:T(8,128)(2,1)}), bf16[32,2880]{1,0:T(8,128)(2,1)}) %reduce-scatter.2.cloned.1.call-update) | async-done | bytes 184336 | tf_op jit(solution)/shard_map/reduce_scatter | solution.py:146
  270.2 32.6 %all-reduce.5.cloned.1.call-done = bf16[32,2880]{1,0:T(8,128)(2,1)} async-done(((bf16[32,2880]{1,0:T(8,128)(2,1)}), bf16[32,2880]{1,0:T(8,128)(2,1)}) %all-reduce.5.cloned.1.call-update) | async-done | bytes 184336 | tf_op jit(solution)/shard_map/psum | solution.py:147
  302.9 1.3 multiply_reduce_fusion.1
  304.2 1.7 multiply_convert_fusion
  305.9 1.7 fusion.85
  307.6 1.2 fusion.81
  308.8 0.6 copy.133
  (88 shorter events, 3.6 us)
Async XLA Ops:
  7.2 89.8 %copy-start = (bf16[512,2880]{0,1:T(8,128)(2,1)S(1)}, bf16[512,2880]{0,1:T(8,128)(2,1)}, u32[]{:S(2)}) copy-start(bf16[512,2880]{0,1:T(8,128)(2,1)} %param.33) | copy-start | bytes 8847364
  54.6 5.0 %copy-start.7 = (pred[8,8,4,324]{3,1,2,0:T(8,128)(4,1)}, pred[8,8,4,324]{3,1,2,0:T(8,128)(4,1)S(1)}, u32[]{:S(2)}) copy-start(pred[8,8,4,324]{3,1,2,0:T(8,128)(4,1)S(1)} %pad_add_fusion) | copy-start | bytes 248836
  56.7 1.7 copy-start.1
  56.7 2.9 copy-start.5
  56.7 11.4 %copy-start.11 = (bf16[4,8,128]{2,1,0:T(8,128)(2,1)S(1)}, bf16[4,8,128]{2,1,0:T(8,128)(2,1)}, u32[]{:S(2)}) copy-start(bf16[4,8,128]{2,1,0:T(8,128)(2,1)} %param.24) | copy-start | bytes 24580
  60.4 12.0 %copy-start.6 = (f32[8,2,8,4,4]{2,4,3,1,0:T(4,128)S(1)}, f32[8,2,8,4,4]{2,4,3,1,0:T(4,128)}, u32[]{:S(2)}) copy-start(f32[8,2,8,4,4]{2,4,3,1,0:T(4,128)} %copy-done.5) | copy-start | bytes 24580
  62.6 16.1 %all-to-all-start.1 = ((f32[8,1,512]{2,1,0:T(1,128)}), f32[8,1,512]{2,1,0:T(1,128)S(1)}, u32[]{:S(2)}, u32[]{:S(2)}) async-start(f32[8,1,512]{2,1,0:T(1,128)} %reshape.201), calls=%async_computation.1 | async-start | bytes 32768 | tf_op jit(solution)/shard_map/all_to_all | solution.py:116
  72.4 3.9 %copy-start.14 = (f32[8]{0:T(128)S(1)}, f32[8]{0:T(128)}, u32[]{:S(2)}) copy-start(f32[8]{0:T(128)} %param.32) | copy-start | bytes 100
  78.7 14.3 %all-to-all-start = ((bf16[8,2,8192]{2,1,0:T(2,128)(2,1)}), bf16[8,2,8192]{2,1,0:T(2,128)(2,1)}, u32[]{:S(2)}, u32[]{:S(2)}) async-start(bf16[8,2,8192]{2,1,0:T(2,128)(2,1)} %reshape.199), calls=%async_computation | async-start | bytes 524288 | tf_op jit(solution)/shard_map/all_to_all | solution.py:115
  84.7 44.0 %all-reduce.3.cloned.1.call-start = ((), (), s32[]{:S(2)}) async-start(), calls=%async_computation.3 | async-start | bytes 376832 | tf_op jit(solution)/shard_map/psum | solution.py:125
  86.4 42.3 %copy-start.2 = (bf16[4,8,2880]{2,1,0:T(8,128)(2,1)S(1)}, bf16[4,8,2880]{2,1,0:T(8,128)(2,1)}, u32[]{:S(2)}) copy-start(bf16[4,8,2880]{2,1,0:T(8,128)(2,1)} %param.21) | copy-start | bytes 552964
  86.6 43.2 %copy-start.10 = (f32[2880]{0:T(1024)S(1)}, f32[2880]{0:T(1024)}, u32[]{:S(2)}) copy-start(f32[2880]{0:T(1024)} %param.34) | copy-start | bytes 34564
  87.1 44.5 %copy-start.12 = (s32[4,8,4]{1,2,0:T(4,128)S(1)}, s32[4,8,4]{1,2,0:T(4,128)}, u32[]{:S(2)}) copy-start(s32[4,8,4]{1,2,0:T(4,128)} %param.31) | copy-start | bytes 1540
  87.1 44.6 %copy-start.8 = (bf16[2880,16]{0,1:T(8,128)(2,1)S(1)}, bf16[2880,16]{0,1:T(8,128)(2,1)}, u32[]{:S(2)}) copy-start(bf16[2880,16]{0,1:T(8,128)(2,1)} %param.35) | copy-start | bytes 276484
  98.6 76.6 %all-gather.3.cloned.1.call-start = ((), (), s32[]{:S(2)}) async-start(), calls=%async_computation.4 | async-start | bytes 1695744 | tf_op jit(solution)/shard_map/all_gather | solution.py:134
  131.5 138.7 %reduce-scatter.2.cloned.1.call-start = ((), (), s32[]{:S(2)}) async-start(), calls=%async_computation.5 | async-start | bytes 1695744 | tf_op jit(solution)/shard_map/reduce_scatter | solution.py:146
  175.3 5.0 %copy-start.13 = (bf16[256,2880]{1,0:T(8,128)(2,1)S(1)}, bf16[256,2880]{1,0:T(8,128)(2,1)}, u32[]{:S(2)}) copy-start(bf16[256,2880]{1,0:T(8,128)(2,1)} %all-gather.3.cloned.1.call-done) | copy-start | bytes 4423684
  195.3 107.5 %copy-start.3 = (bf16[32,2880]{1,0:T(8,128)(2,1)S(1)}, bf16[32,2880]{1,0:T(8,128)(2,1)}, u32[]{:S(2)}) copy-start(bf16[32,2880]{1,0:T(8,128)(2,1)} %all-reduce.3.cloned.1.call-done) | copy-start | bytes 552964
  195.3 108.8 %copy-start.9 = (f32[2880]{0:T(1024)S(1)}, f32[2880]{0:T(1024)}, u32[]{:S(2)}) copy-start(f32[2880]{0:T(1024)} %param.39) | copy-start | bytes 34564
  206.4 96.4 %all-reduce.5.cloned.1.call-start = ((), (), s32[]{:S(2)}) async-start(), calls=%async_computation.6 | async-start | bytes 376832 | tf_op jit(solution)/shard_map/psum | solution.py:147
  302.9 4.8 %copy-start.4 = (bf16[2880,512]{1,0:T(8,128)(2,1)S(1)}, bf16[2880,512]{1,0:T(8,128)(2,1)}, u32[]{:S(2)}) copy-start(bf16[2880,512]{1,0:T(8,128)(2,1)} %param.40) | copy-start | bytes 8847364
Sparse Core Ops, SparseCore 0:
  98.8 29.8 all-reduce.2
  131.6 43.5 all-gather.2
  206.6 63.5 reduce-scatter.1
  272.4 30.4 all-reduce.4
where the time goes:
time: 317 us; the launch traced here: 316 us
  waiting for transfers between devices  144 us (45%)
  blocking collectives  65.4 us (21%)
  matrix products  42.8 us (14%)
  local copies, waits for them, and re-layouts  19.6 us (6%)
  other arithmetic  18.8 us (6%)
  between operations  14.2 us (4%)
  starting transfers between devices  11.6 us (4%)
    reduce_scatter x1, waiting for transfers between devices, local(): lax.psum_scatter(moe.astype(BF), 'req', scatter_dimension=0, tiled=True)  63.7 us
    all_gather x1, blocking collectives, local(): q_all = lax.all_gather(q, 'req', axis_index_groups=groups)  34.5 us
    psum x1, waiting for transfers between devices, local(): moe = lax.psum(moe, 'tp').astype(F32)  32.6 us
    all_gather x1, blocking collectives, local(): gates_all = lax.all_gather(gates, 'req', tiled=True)  30.8 us
    psum x1, waiting for transfers between devices, local(): lax.psum(projected.astype(BF), 'tp').astype(F32)  29.9 us
    dot_general x2, matrix products, local(): moe = moe + jnp.dot(hidden, expert_down[s], preferred_element_type=F32)  21.7 us
    all_gather x1, waiting for transfers between devices, local(): h2_all = lax.all_gather(h2, 'req', tiled=True)  11.5 us
    dot_general x2, matrix products, local(): jnp.dot(h2_all, expert_gate[s], preferred_element_type=F32)  9.4 us
  transfers between devices with their start and end apart: 6, of which 5 were waited for; matrix products, arithmetic and copies ran while one was open for 5% of the time, Pallas kernels for 0%

commit v1 on v0

--- a/solution.py
+++ b/solution.py
@@ -131,8 +131,11 @@
     masked = jnp.where(hot > 0, logits, NEG)
     raw = jnp.where(hot > 0, jnp.exp(masked - jnp.max(masked, axis=-1, keepdims=True)), 0.0)
     gates = raw / jnp.sum(raw, axis=-1, keepdims=True)
-    h2_all = lax.all_gather(h2, "req", tiled=True)
-    gates_all = lax.all_gather(gates, "req", tiled=True)
+    h2_all, gates_all = jnp.split(
+        lax.all_gather(jnp.concatenate([h2, gates], axis=1), "req", axis=0, tiled=True),
+        [h2.shape[1]],
+        axis=1,
+    )
     slabs = expert_gate.shape[0]
     split = slabs * req_count // EXPERTS
     moe = 0.0

time: 317 us -> 337 us (1.063)
  waiting for transfers between devices: 144 us -> 191 us
  blocking collectives: 65.4 us -> 34.5 us
    all_gather x1, waiting for transfers between devices: 11.5 us -> 59.1 us  [local(): lax.all_gather(jnp.concatenate([h2, gates], axis=1), 'req', axis=0, tiled...]
    all_gather x1 -> x0, blocking collectives: 30.8 us -> none  [local(): gates_all = lax.all_gather(gates, 'req', tiled=True)]
    unnamed x38 -> x37, local copies, waits for them, and re-layouts: 6.82 us -> 6.74 us
  transfers between devices with their start and end apart: 6 -> 6, of which waited for: 5 -> 5; matrix products, arithmetic and copies ran while one was open for 5% -> 4% of each run, Pallas kernels for 0% -> 0%
where the time goes in v1:
time: 337 us; the launch traced here: 336 us
  waiting for transfers between devices  191 us (57%)
  matrix products  44.3 us (13%)
  blocking collectives  34.5 us (10%)
  local copies, waits for them, and re-layouts  20.8 us (6%)
  other arithmetic  19.2 us (6%)
  between operations  14.2 us (4%)
  starting transfers between devices  11.8 us (4%)
    reduce_scatter x1, waiting for transfers between devices, local(): lax.psum_scatter(moe.astype(BF), 'req', scatter_dimension=0, tiled=True)  63.6 us
    all_gather x1, waiting for transfers between devices, local(): lax.all_gather(jnp.concatenate([h2, gates], axis=1), 'req', axis=0, tiled...  59.1 us
    all_gather x1, blocking collectives, local(): q_all = lax.all_gather(q, 'req', axis_index_groups=groups)  34.5 us
    psum x1, waiting for transfers between devices, local(): moe = lax.psum(moe, 'tp').astype(F32)  32.7 us
    psum x1, waiting for transfers between devices, local(): lax.psum(projected.astype(BF), 'tp').astype(F32)  29.9 us
    dot_general x2, matrix products, local(): moe = moe + jnp.dot(hidden, expert_down[s], preferred_element_type=F32)  22.6 us
    dot_general x2, matrix products, local(): jnp.dot(h2_all, expert_gate[s], preferred_element_type=F32)  9.88 us
  transfers between devices with their start and end apart: 6, of which 5 were waited for; matrix products, arithmetic and copies ran while one was open for 4% of the time, Pallas kernels for 0%

profile of v1, /device:TPU:0, one launch (start us, length us, event | category | flops | bytes accessed | tf_op | source)
XLA Modules:
  0.0 335.9 jit_solution(14099005123915770695)
XLA Ops:
  7.2 0.8 broadcast_add_fusion
  8.0 0.8 broadcast_compare_fusion.1
  8.8 0.7 slice_bitcast_fusion.4
  10.1 0.5 select_reduce_fusion.8
  10.7 0.7 select_reduce_fusion.9
  12.0 0.8 reshape.192
  13.1 0.9 reshape.190
  14.3 34.5 %all_gather.6 = bf16[8,4,8,512]{3,2,1,0:T(8,128)(2,1)} all-gather(bf16[1,4,8,512]{3,2,1,0:T(8,128)(2,1)S(1)} %convert_element_type.90), channel_id=1, replica_groups=mesh['req'=8,'tp'=4] {'req'}, dimensions={0}, use_global_device_ids=true | all-gather | bytes 294912 | tf_op jit(solution)/shard_map/all_gather | solution.py:88
  48.8 1.3 reshape.181
  50.1 2.0 pad_maximum_fusion.1
  52.1 2.2 copy.123
  54.6 2.0 fusion.24
  56.7 1.6 copy-done.1
  58.3 1.3 fusion.29
  59.6 0.8 pad_maximum_fusion.3
  60.4 1.3 copy.126
  61.7 0.9 reshape.201
  62.6 5.5 %all-to-all-start.1 = ((f32[8,1,512]{2,1,0:T(1,128)}), f32[8,1,512]{2,1,0:T(1,128)S(1)}, u32[]{:S(2)}, u32[]{:S(2)}) async-start(f32[8,1,512]{2,1,0:T(1,128)} %reshape.201), calls=%async_computation.1 | async-start | bytes 32768 | tf_op jit(solution)/shard_map/all_to_all | solution.py:116
  68.1 2.0 pad_maximum_fusion
  70.1 2.2 copy.116
  72.4 3.9 %divide_convert_fusion = bf16[8,4,8,2,4,64]{5,0,4,1,3,2:T(8,128)(2,1)} fusion(bf16[8,324,2,64,1,1]{1,3,5,4,2,0:T(8,128)(2,1)} %bitcast.185, f32[8,2,8,4,4,324]{5,2,4,3,1,0:T(8,128)} %copy-done.1, f32[8,2,8,4,4]{2,4,3,1,0:T(4,128)S(1)} %copy-done.6, pred[8,8,4,324]{3,1,2,0:T(8,128)(4,1)} %copy-done.7, f32[8,4,8,2,4]{0,4,1,3,2:T(4,128)S(1)} %bitcast_maximum_fusion), kind=kOutput, calls=%fused_computation.59 | convolution fusion | flops 88514560 | bytes 3679232 | tf_op jit(solution)/shard_map/bkjtrs,bskd->jtbkrd/dot_general | solution.py:110
  76.4 1.2 copy.160
  77.7 1.1 reshape.199
  78.8 6.0 %all-to-all-start = ((bf16[8,2,8192]{2,1,0:T(2,128)(2,1)}), bf16[8,2,8192]{2,1,0:T(2,128)(2,1)}, u32[]{:S(2)}, u32[]{:S(2)}) async-start(bf16[8,2,8192]{2,1,0:T(2,128)(2,1)} %reshape.199), calls=%async_computation | async-start | bytes 524288 | tf_op jit(solution)/shard_map/all_to_all | solution.py:115
  84.8 0.5 broadcast.193
  85.3 0.7 reduce.5
  87.2 5.9 %all-to-all-done = bf16[8,2,8192]{2,1,0:T(2,128)(2,1)} async-done(((bf16[8,2,8192]{2,1,0:T(2,128)(2,1)}), bf16[8,2,8192]{2,1,0:T(2,128)(2,1)}, u32[]{:S(2)}, u32[]{:S(2)}) %all-to-all-start) | async-done | bytes 262176 | tf_op jit(solution)/shard_map/all_to_all | solution.py:115
  93.1 2.1 reshape.200
  95.2 1.7 multiply_reduce_fusion
  97.1 1.6 convolution_convert_fusion
  98.9 29.9 %all-reduce.3.cloned.1.call-done = bf16[32,2880]{1,0:T(8,128)(2,1)} async-done(((bf16[32,2880]{1,0:T(8,128)(2,1)}), bf16[32,2880]{1,0:T(8,128)(2,1)}) %all-reduce.3.cloned.1.call-update) | async-done | bytes 184336 | tf_op jit(solution)/shard_map/psum | solution.py:125
  128.8 1.1 multiply_reduce_fusion.2
  129.9 1.3 fusion.163
  131.5 1.0 fusion.161
  132.5 0.8 pad_maximum_fusion.2
  133.6 59.1 %all-gather.2.cloned.1.call-done = f32[256,2896]{1,0:T(8,128)} async-done(((f32[32,2896]{1,0:T(8,128)}), f32[256,2896]{1,0:T(8,128)}) %all-gather.2.cloned.1.call-update) | async-done | bytes 2965520 | tf_op jit(solution)/shard_map/all_gather | solution.py:135
  192.7 1.0 split.9
  193.9 5.5 %fusion.48 = f32[256,720]{0,1:T(8,128)} fusion(bf16[2,2880,720]{1,2,0:T(8,128)(2,1)} %param.36, f32[256,2896]{1,0:T(8,128)} %all-gather.2.cloned.1.call-done), kind=kOutput, calls=%fused_computation.40 | convolution fusion | flops 1061867520 | bytes 6483968 | tf_op jit(solution)/shard_map/dot_general | solution.py:145
  199.4 4.4 %fusion.58 = f32[256,720]{0,1:T(8,128)} fusion(bf16[2,2880,720]{1,2,0:T(8,128)(2,1)} %param.36, f32[256,2896]{1,0:T(8,128)S(1)} %copy-done.12), kind=kOutput, calls=%fused_computation.42 | convolution fusion | flops 1061867520 | bytes 6483968 | tf_op jit(solution)/shard_map/dot_general | solution.py:145
  203.8 11.1 %fusion = f32[256,2880]{1,0:T(8,128)} fusion(bf16[2,720,2880]{2,1,0:T(8,128)(2,1)} %param.38, f32[256,720]{0,1:T(8,128)} %fusion.58, bf16[2,2880,720]{1,2,0:T(8,128)(2,1)} %param.37, f32[256,2896]{1,0:T(8,128)} %all-gather.2.cloned.1.call-done, f32[256]{0:T(256)S(1)} %get-tuple-element.22), kind=kOutput, calls=%fused_computation | convolution fusion | flops 2125209600 | bytes 13673472 | tf_op jit(solution)/shard_map/dot_general | solution.py:148
  214.9 11.5 %fusion.21 = bf16[256,2880]{1,0:T(8,128)(2,1)} fusion(f32[256,2880]{1,0:T(8,128)} %fusion, bf16[2,720,2880]{2,1,0:T(8,128)(2,1)} %param.38, f32[256,720]{0,1:T(8,128)} %fusion.48, bf16[2,2880,720]{1,2,0:T(8,128)(2,1)} %param.37, f32[256,2896]{1,0:T(8,128)} %all-gather.2.cloned.1.call-done, f32[256]{0:T(256)S(1)} %get-tuple-element.21), kind=kOutput, calls=%fused_computation.19 | convolution fusion | flops 2126684160 | bytes 15213568 | tf_op jit(solution)/shard_map/dot_general | solution.py:148
  226.5 63.6 %reduce-scatter.2.cloned.1.call-done = bf16[32,2880]{1,0:T(8,128)(2,1)} async-done(((bf16[256,2880]{1,0:T(8,128)(2,1)}), bf16[32,2880]{1,0:T(8,128)(2,1)}) %reduce-scatter.2.cloned.1.call-update) | async-done | bytes 184336 | tf_op jit(solution)/shard_map/reduce_scatter | solution.py:149
  290.1 32.7 %all-reduce.5.cloned.1.call-done = bf16[32,2880]{1,0:T(8,128)(2,1)} async-done(((bf16[32,2880]{1,0:T(8,128)(2,1)}), bf16[32,2880]{1,0:T(8,128)(2,1)}) %all-reduce.5.cloned.1.call-update) | async-done | bytes 184336 | tf_op jit(solution)/shard_map/psum | solution.py:150
  322.8 1.3 multiply_reduce_fusion.1
  324.1 1.7 multiply_convert_fusion
  325.8 1.7 fusion.117
  327.5 1.2 fusion.113
  328.7 0.6 copy.135
  (88 shorter events, 4.7 us)
Async XLA Ops:
  7.2 89.9 %copy-start = (bf16[512,2880]{0,1:T(8,128)(2,1)S(1)}, bf16[512,2880]{0,1:T(8,128)(2,1)}, u32[]{:S(2)}) copy-start(bf16[512,2880]{0,1:T(8,128)(2,1)} %param.33) | copy-start | bytes 8847364
  54.6 5.0 %copy-start.7 = (pred[8,8,4,324]{3,1,2,0:T(8,128)(4,1)}, pred[8,8,4,324]{3,1,2,0:T(8,128)(4,1)S(1)}, u32[]{:S(2)}) copy-start(pred[8,8,4,324]{3,1,2,0:T(8,128)(4,1)S(1)} %pad_add_fusion) | copy-start | bytes 248836
  56.7 1.7 copy-start.1
  56.7 2.9 copy-start.5
  56.7 11.4 %copy-start.10 = (bf16[4,8,128]{2,1,0:T(8,128)(2,1)S(1)}, bf16[4,8,128]{2,1,0:T(8,128)(2,1)}, u32[]{:S(2)}) copy-start(bf16[4,8,128]{2,1,0:T(8,128)(2,1)} %param.24) | copy-start | bytes 24580
  60.4 12.0 %copy-start.6 = (f32[8,2,8,4,4]{2,4,3,1,0:T(4,128)S(1)}, f32[8,2,8,4,4]{2,4,3,1,0:T(4,128)}, u32[]{:S(2)}) copy-start(f32[8,2,8,4,4]{2,4,3,1,0:T(4,128)} %copy-done.5) | copy-start | bytes 24580
  62.6 16.2 %all-to-all-start.1 = ((f32[8,1,512]{2,1,0:T(1,128)}), f32[8,1,512]{2,1,0:T(1,128)S(1)}, u32[]{:S(2)}, u32[]{:S(2)}) async-start(f32[8,1,512]{2,1,0:T(1,128)} %reshape.201), calls=%async_computation.1 | async-start | bytes 32768 | tf_op jit(solution)/shard_map/all_to_all | solution.py:116
  72.4 3.9 %copy-start.14 = (f32[8]{0:T(128)S(1)}, f32[8]{0:T(128)}, u32[]{:S(2)}) copy-start(f32[8]{0:T(128)} %param.32) | copy-start | bytes 100
  72.4 4.0 %copy-start.11 = (s32[4,8,4]{1,2,0:T(4,128)S(1)}, s32[4,8,4]{1,2,0:T(4,128)}, u32[]{:S(2)}) copy-start(s32[4,8,4]{1,2,0:T(4,128)} %param.31) | copy-start | bytes 1540
  78.8 14.3 %all-to-all-start = ((bf16[8,2,8192]{2,1,0:T(2,128)(2,1)}), bf16[8,2,8192]{2,1,0:T(2,128)(2,1)}, u32[]{:S(2)}, u32[]{:S(2)}) async-start(bf16[8,2,8192]{2,1,0:T(2,128)(2,1)} %reshape.199), calls=%async_computation | async-start | bytes 524288 | tf_op jit(solution)/shard_map/all_to_all | solution.py:115
  84.8 44.0 %all-reduce.3.cloned.1.call-start = ((), (), s32[]{:S(2)}) async-start(), calls=%async_computation.3 | async-start | bytes 376832 | tf_op jit(solution)/shard_map/psum | solution.py:125
  86.5 42.3 %copy-start.2 = (bf16[4,8,2880]{2,1,0:T(8,128)(2,1)S(1)}, bf16[4,8,2880]{2,1,0:T(8,128)(2,1)}, u32[]{:S(2)}) copy-start(bf16[4,8,2880]{2,1,0:T(8,128)(2,1)} %param.21) | copy-start | bytes 552964
  86.7 43.2 %copy-start.9 = (f32[2880]{0:T(1024)S(1)}, f32[2880]{0:T(1024)}, u32[]{:S(2)}) copy-start(f32[2880]{0:T(1024)} %param.34) | copy-start | bytes 34564
  87.2 42.7 %copy-start.13 = (bf16[2880,16]{0,1:T(8,128)(2,1)S(1)}, bf16[2880,16]{0,1:T(8,128)(2,1)}, u32[]{:S(2)}) copy-start(bf16[2880,16]{0,1:T(8,128)(2,1)} %param.35) | copy-start | bytes 276484
  98.8 93.9 %all-gather.2.cloned.1.call-start = ((), (), s32[]{:S(2)}) async-start(), calls=%async_computation.4 | async-start | bytes 3391488 | tf_op jit(solution)/shard_map/all_gather | solution.py:135
  133.4 156.7 %reduce-scatter.2.cloned.1.call-start = ((), (), s32[]{:S(2)}) async-start(), calls=%async_computation.5 | async-start | bytes 1695744 | tf_op jit(solution)/shard_map/reduce_scatter | solution.py:149
  193.9 5.5 %copy-start.12 = (f32[256,2896]{1,0:T(8,128)S(1)}, f32[256,2896]{1,0:T(8,128)}, u32[]{:S(2)}) copy-start(f32[256,2896]{1,0:T(8,128)} %all-gather.2.cloned.1.call-done) | copy-start | bytes 8896516
  214.9 107.8 %copy-start.3 = (bf16[32,2880]{1,0:T(8,128)(2,1)S(1)}, bf16[32,2880]{1,0:T(8,128)(2,1)}, u32[]{:S(2)}) copy-start(bf16[32,2880]{1,0:T(8,128)(2,1)} %all-reduce.3.cloned.1.call-done) | copy-start | bytes 552964
  214.9 109.1 %copy-start.8 = (f32[2880]{0:T(1024)S(1)}, f32[2880]{0:T(1024)}, u32[]{:S(2)}) copy-start(f32[2880]{0:T(1024)} %param.39) | copy-start | bytes 34564
  226.4 96.3 %all-reduce.5.cloned.1.call-start = ((), (), s32[]{:S(2)}) async-start(), calls=%async_computation.6 | async-start | bytes 376832 | tf_op jit(solution)/shard_map/psum | solution.py:150
  322.8 4.8 %copy-start.4 = (bf16[2880,512]{1,0:T(8,128)(2,1)S(1)}, bf16[2880,512]{1,0:T(8,128)(2,1)}, u32[]{:S(2)}) copy-start(bf16[2880,512]{1,0:T(8,128)(2,1)} %param.40) | copy-start | bytes 8847364
Sparse Core Ops, SparseCore 0:
  98.9 29.8 all-reduce.2
  133.5 59.1 all-gather.1
  226.6 63.4 reduce-scatter.1
  292.2 30.4 all-reduce.4
